TPU v7x, 512 devices: a whole 4x8x8 slice. The times are simulated.
512 devices in a mesh: dp: 8 (over x, core), ctx: 64 (over y, z).
Axes of the slice: x: 4, y: 8, z: 8, core: 2. Of those that a mesh axis runs over, the one named last changes fastest.
Arguments:
- token_ids: int32 [8, 8192], P('dp', 'ctx'), may hold values from 0 to 7
- queries: bfloat16 [8, 8192, 4096], P('dp', 'ctx'), may hold values from -6 to 6
- gated_values: bfloat16 [8, 8192, 4096], P('dp', 'ctx'), may hold values from -6 to 6
- out_grad: bfloat16 [8, 8192, 4096], P('dp', 'ctx'), may hold values from -6 to 6
- filters: bfloat16 [4096, 128], P('ctx'), may hold values from -0.5 to 0.5
Outputs:
- value_grad: bfloat16 [8, 8192, 4096], P('dp', 'ctx')
- filter_grad: float32 [4096, 128], P('ctx')
Inputs may be any that keep to these rules, and one draw needn't show every extreme that they name: `token_ids`: ids 0 to 3 are upper-case bases, 4 to 7 lower-case bases.
All inputs are finite; a program needn't handle non-finite values.
Results may differ from a plain program's by a relative error of at most 0.0049.
Values may be sent and summed in bfloat16 or wider, within the bound.
A program may use at most 64 MiB of HBM per device.

v0:
```python
import jax
import jax.numpy as jnp
import numpy as np
from jax import lax
from jax.sharding import PartitionSpec as P


def tables(span):
    half = span // 2
    angle = np.pi * (2 * np.arange(half)[:, None] + 1) * np.arange(span)[None, :] / span
    wave = np.concatenate([np.cos(angle), np.sin(angle)], axis=0)
    high = wave.astype(jnp.bfloat16)
    low = (wave - high.astype(np.float64)).astype(jnp.bfloat16)
    return (high, low)


def mul(a, b):
    return jnp.dot(a, b, preferred_element_type=jnp.float32)


def body(token_ids, queries, gated_values, out_grad, filters):
    dp, ctx = (lax.axis_size("dp"), lax.axis_size("ctx"))
    weight = jnp.where(token_ids < 4, 1.0, 0.1).astype(jnp.float32)
    cotangent = (
        weight[:, :, None] * out_grad.astype(jnp.float32) * queries.astype(jnp.float32)
    ).astype(jnp.bfloat16)[0]
    rows = cotangent.shape[0]
    factor_tok = float(dp * ctx * rows) ** (-0.5)
    taps = lax.all_gather(filters, "ctx", axis=0, tiled=True)
    after = lax.ppermute(cotangent, "ctx", [(i, i - 1) for i in range(1, ctx)])
    high, low = (jnp.asarray(t) for t in tables(2 * rows))

    def forward(x):
        n = x.shape[0]
        wave = mul(high[:, :n], x) + mul(low[:, :n], x)
        return (wave[:rows], wave[rows:])

    def backward(re, im):
        both = jnp.concatenate([re, im], axis=0) * (1.0 / rows)
        top = both.astype(jnp.bfloat16)
        rest = (both - top.astype(jnp.float32)).astype(jnp.bfloat16)
        up, down = (high[:, :rows].T, low[:, :rows].T)
        return mul(up, top) + (mul(up, rest) + mul(down, top))

    cot_cos, cot_sin = forward(jnp.concatenate([cotangent, after], axis=0))

    def correlate(x):
        x_cos, x_sin = forward(x)
        return backward(cot_cos * x_cos + cot_sin * x_sin, cot_sin * x_cos - cot_cos * x_sin)

    tap_part = correlate(gated_values[0]).T * factor_tok
    filter_grad = lax.psum(lax.psum_scatter(tap_part, "ctx", scatter_dimension=0, tiled=True), "dp")
    value_grad = correlate(taps.T).astype(jnp.bfloat16)[None]
    return (value_grad, filter_grad)


def solution(mesh):
    return jax.shard_map(
        body,
        mesh=mesh,
        in_specs=(
            P("dp", "ctx"),
            P("dp", "ctx", None),
            P("dp", "ctx", None),
            P("dp", "ctx", None),
            P("ctx", None),
        ),
        out_specs=(P("dp", "ctx", None), P("ctx", None)),
        check_vma=False,
    )
```

profile of v0, /device:TPU:16, one launch (start us, length us, event | category | flops | bytes accessed | tf_op | source)
XLA Modules:
  0.0 386.2 jit_solution(3704554985823753769)
XLA Ops:
  7.2 0.0 copy-start
  7.2 0.0 copy-start.5
  7.2 0.0 all-gather.2.cloned.1.call-start
  7.2 0.7 all-gather.2.cloned.1.call-update
  7.9 0.0 reduce-scatter.2.cloned.1.call-start
  8.0 0.7 fusion.25
  8.6 1.9 fusion.13
  10.6 0.0 copy-start.4
  10.6 11.0 %collective-permute-start = (bf16[128,4096]{1,0:T(8,128)(2,1)S(1)}, bf16[128,4096]{1,0:T(8,128)(2,1)S(1)}, u32[]{:S(2)}, u32[]{:S(2)}) collective-permute-start(bf16[128,4096]{1,0:T(8,128)(2,1)S(1)} %fusion.13), channel_id=1, source_target_pairs={{1,0},{2,1},{3,2},{4,3},{5,4},{6,5},{7,6},{8,7},{9,8},{10,9},{11,1... | collective-permute-start | bytes 3145736 | tf_op jit(solution)/shard_map/ppermute | solution.py:30
  21.6 0.0 copy-done.5
  21.6 0.7 fusion.40
  22.3 0.0 copy-done.4
  22.3 0.7 fusion.39
  23.0 0.0 copy-done
  23.0 0.7 fusion.15
  23.7 0.0 copy-start.7
  23.7 2.7 convolution_add_fusion.2
  26.4 0.0 copy-start.6
  26.4 17.9 %collective-permute-done = bf16[128,4096]{1,0:T(8,128)(2,1)S(1)} collective-permute-done((bf16[128,4096]{1,0:T(8,128)(2,1)S(1)}, bf16[128,4096]{1,0:T(8,128)(2,1)S(1)}, u32[]{:S(2)}, u32[]{:S(2)}) %collective-permute-start) | collective-permute-done | bytes 1048608 | tf_op jit(solution)/shard_map/ppermute | solution.py:30
  44.3 0.0 copy-done.7
  44.3 0.7 convolution_add_fusion.1
  45.0 0.0 copy-done.6
  45.0 2.7 fusion.1
  47.7 49.9 %all-gather.2.cloned.1.call-done = bf16[4096,128]{1,0:T(8,128)(2,1)} async-done(((bf16[64,128]{1,0:T(8,128)(2,1)}), bf16[4096,128]{1,0:T(8,128)(2,1)}) %all-gather.2.cloned.1.call-update) | async-done | bytes 1048592 | tf_op jit(solution)/shard_map/all_gather | solution.py:29
  97.6 0.0 copy-start.3
  97.6 2.0 fusion.38
  99.6 0.0 copy-done.3
  99.6 0.0 copy-start.2
  99.6 2.7 convolution_add_fusion.3
  102.4 0.7 copy-done.2
  103.1 6.1 %multiply_add_fusion = (f32[128,4096]{1,0:T(8,128)S(1)}, f32[128,4096]{1,0:T(8,128)S(1)}, f32[128,4096]{1,0:T(8,128)S(1)}, f32[128,4096]{1,0:T(8,128)}) fusion(f32[256,4096]{1,0:T(8,128)S(1)} %copy-done.2, f32[256,4096]{1,0:T(8,128)} %fusion.1, f32[256,4096]{1,0:T(8,128)} %convolution_add_fusion.3), kind=kLoop, calls=%fused_computation.22 | loop fusion | flops 6291456 | bytes 20971520 | tf_op jit(solution)/shard_map/add | solution.py:49
  109.2 0.8 fusion.10
  110.0 0.8 fusion.23
  110.7 2.1 fusion.3
  112.8 0.0 reduce-scatter.2.cloned.1.call-update
  112.9 0.0 copy-start.1
  112.9 2.5 fusion.9
  115.4 0.0 copy-done.1
  115.4 0.8 fusion.19
  116.2 1.9 fusion.6
  118.1 2.3 copy.9
  120.4 234.3 %reduce-scatter.2.cloned.1.call-done = f32[64,128]{1,0:T(8,128)} async-done(((f32[4096,128]{1,0:T(8,128)}), f32[64,128]{1,0:T(8,128)}) %reduce-scatter.2.cloned.1.call-update) | async-done | bytes 32784 | tf_op jit(solution)/shard_map/reduce_scatter | solution.py:52
  354.7 24.7 %psum.7 = f32[64,128]{1,0:T(8,128)} all-reduce(f32[64,128]{1,0:T(8,128)} %reduce-scatter.2.cloned.1.call-done), channel_id=1, replica_groups=mesh['dp'=8,'ctx'=64] {'dp'}, use_global_device_ids=true, to_apply=%region_1.2 | all-reduce | flops 8192 | bytes 65536 | tf_op jit(solution)/shard_map/psum | solution.py:52
Async XLA Ops:
  7.2 15.8 %copy-start = (bf16[1,128,4096]{2,1,0:T(8,128)(2,1)S(1)}, bf16[1,128,4096]{2,1,0:T(8,128)(2,1)}, u32[]{:S(2)}) copy-start(bf16[1,128,4096]{2,1,0:T(8,128)(2,1)} %param.9) | copy-start | bytes 3145732
  7.2 14.4 %copy-start.5 = (bf16[256,128]{1,0:T(8,128)(2,1)S(1)}, bf16[256,128]{1,0:T(8,128)(2,1)}, u32[]{:S(2)}) copy-start(bf16[256,128]{1,0:T(8,128)(2,1)} %constant.22) | copy-start | bytes 196612
  7.2 90.4 %all-gather.2.cloned.1.call-start = ((), (), s32[]{:S(2)}) async-start(), calls=%async_computation.1 | async-start | bytes 1064960 | tf_op jit(solution)/shard_map/all_gather | solution.py:29
  7.9 346.8 %reduce-scatter.2.cloned.1.call-start = ((), (), s32[]{:S(2)}) async-start(), calls=%async_computation.2 | async-start | bytes 2129920 | tf_op jit(solution)/shard_map/reduce_scatter | solution.py:52
  10.6 11.7 %copy-start.4 = (bf16[256,128]{1,0:T(8,128)(2,1)S(1)}, bf16[256,128]{1,0:T(8,128)(2,1)}, u32[]{:S(2)}) copy-start(bf16[256,128]{1,0:T(8,128)(2,1)} %constant.20) | copy-start | bytes 196612
  10.6 33.7 %collective-permute-start = (bf16[128,4096]{1,0:T(8,128)(2,1)S(1)}, bf16[128,4096]{1,0:T(8,128)(2,1)S(1)}, u32[]{:S(2)}, u32[]{:S(2)}) collective-permute-start(bf16[128,4096]{1,0:T(8,128)(2,1)S(1)} %fusion.13), channel_id=1, source_target_pairs={{1,0},{2,1},{3,2},{4,3},{5,4},{6,5},{7,6},{8,7},{9,8},{10,9},{11,1... | collective-permute-start | bytes 3145736 | tf_op jit(solution)/shard_map/ppermute | solution.py:30
  23.7 20.6 %copy-start.7 = (bf16[256,128]{1,0:T(8,128)(2,1)S(1)}, bf16[256,128]{1,0:T(8,128)(2,1)}, u32[]{:S(2)}) copy-start(bf16[256,128]{1,0:T(8,128)(2,1)} %constant.21) | copy-start | bytes 196612
  26.4 18.6 %copy-start.6 = (bf16[256,128]{1,0:T(8,128)(2,1)S(1)}, bf16[256,128]{1,0:T(8,128)(2,1)}, u32[]{:S(2)}) copy-start(bf16[256,128]{1,0:T(8,128)(2,1)} %constant.23) | copy-start | bytes 196612
  97.6 2.0 copy-start.3
  99.6 3.5 copy-start.2
  112.9 2.5 copy-start.1
Sparse Core Ops, SparseCore 0:
  11.0 86.4 all-gather.1
  113.0 241.6 reduce-scatter.1
where the time goes:
time: 387 us; the launch traced here: 386 us
  waiting for transfers between devices  303 us (78%)
  blocking collectives  24.7 us (6%)
  matrix products  21.8 us (6%)
  between operations  14.2 us (4%)
  starting transfers between devices  11 us (3%)
  other arithmetic  8.73 us (2%)
    reduce_scatter x1, waiting for transfers between devices, body(): lax.psum_scatter(tap_part, 'ctx', scatter_dimension=0, tiled=True)  234 us
    all_gather x1, waiting for transfers between devices, body(): taps = lax.all_gather(filters, 'ctx', axis=0, tiled=True)  49.9 us
    psum x1, blocking collectives, body(): lax.psum(lax.psum_scatter(tap_part, 'ctx', scatter_dimension=0, tiled=Tru...  24.7 us
    dot_general x14, matrix products, mul(): return jnp.dot(a, b, preferred_element_type=jnp.float32)  21.8 us
    ppermute x1, waiting for transfers between devices, body(): after = lax.ppermute(cotangent, 'ctx', [(i, i - 1) for i in range(1, ctx)])  17.9 us
    ppermute x1, starting transfers between devices, body(): after = lax.ppermute(cotangent, 'ctx', [(i, i - 1) for i in range(1, ctx)])  11 us
  transfers between devices with their start and end apart: 3, of which 3 were waited for; matrix products, arithmetic and copies ran while one was open for 5% of the time, Pallas kernels for 0%

commit v1 on v0

--- a/solution.py
+++ b/solution.py
@@ -26,7 +26,19 @@
     ).astype(jnp.bfloat16)[0]
     rows = cotangent.shape[0]
     factor_tok = float(dp * ctx * rows) ** (-0.5)
-    taps = lax.all_gather(filters, "ctx", axis=0, tiled=True)
+    passed = lax.axis_index("ctx")
+    all_rows = lax.axis_size("ctx")
+    plain, new = (all_rows, passed)
+    taps, block_now = (filters, 1)
+    while block_now < plain:
+        vals = []
+        for at in range(plain):
+            vals.append((at, at ^ block_now))
+        reached = lax.ppermute(taps, axis_name="ctx", perm=vals)
+        g_now = jnp.concatenate([taps, reached], 0)
+        h_now = jnp.concatenate([reached, taps], 0)
+        taps = jnp.where(new & block_now == 0, g_now, h_now)
+        block_now = 2 * block_now
     after = lax.ppermute(cotangent, "ctx", [(i, i - 1) for i in range(1, ctx)])
     high, low = (jnp.asarray(t) for t in tables(2 * rows))
 

time: 387 us -> 395 us (1.021)
  starting transfers between devices: 11 us -> 35 us
  waiting for transfers between devices: 303 us -> 279 us
  matrix products: 21.8 us -> 29.4 us
    all_gather x1 -> x0, waiting for transfers between devices: 49.9 us -> none  [body(): taps = lax.all_gather(filters, 'ctx', axis=0, tiled=True)]
    ppermute x0 -> x6, waiting for transfers between devices: none -> 39.4 us  [body(): reached = lax.ppermute(taps, axis_name='ctx', perm=vals)]
    ppermute x0 -> x6, starting transfers between devices: none -> 32.8 us  [body(): reached = lax.ppermute(taps, axis_name='ctx', perm=vals)]
    ppermute x1, waiting for transfers between devices: 17.9 us -> 0.01 us  [body(): after = lax.ppermute(cotangent, 'ctx', [(i, i - 1) for i in range(1, ctx)])]
    ppermute x1, starting transfers between devices: 11 us -> 2.18 us  [body(): after = lax.ppermute(cotangent, 'ctx', [(i, i - 1) for i in range(1, ctx)])]
    dot_general x14, matrix products: 21.8 us -> 29.4 us  [mul(): return jnp.dot(a, b, preferred_element_type=jnp.float32)]
    reduce_scatter x1, waiting for transfers between devices: 234 us -> 239 us  [body(): lax.psum_scatter(tap_part, 'ctx', scatter_dimension=0, tiled=True)]
  transfers between devices with their start and end apart: 3 -> 8, of which waited for: 3 -> 6; matrix products, arithmetic and copies ran while one was open for 5% -> 6% of each run, Pallas kernels for 0% -> 0%
where the time goes in v1:
time: 395 us
  waiting for transfers between devices  279 us (71%)
  starting transfers between devices  35 us (9%)
  matrix products  29.4 us (7%)
  blocking collectives  24.7 us (6%)
  between operations  14.2 us (4%)
  other arithmetic  9.84 us (2%)
    reduce_scatter x1, waiting for transfers between devices, body(): lax.psum_scatter(tap_part, 'ctx', scatter_dimension=0, tiled=True)  239 us
    ppermute x6, waiting for transfers between devices, body(): reached = lax.ppermute(taps, axis_name='ctx', perm=vals)  39.4 us
    ppermute x6, starting transfers between devices, body(): reached = lax.ppermute(taps, axis_name='ctx', perm=vals)  32.8 us
    dot_general x14, matrix products, mul(): return jnp.dot(a, b, preferred_element_type=jnp.float32)  29.4 us
    psum x1, blocking collectives, body(): lax.psum(lax.psum_scatter(tap_part, 'ctx', scatter_dimension=0, tiled=Tru...  24.7 us
  transfers between devices with their start and end apart: 8, of which 6 were waited for; matrix products, arithmetic and copies ran while one was open for 6% of the time, Pallas kernels for 0%

profile of v1, /device:TPU:16, one launch (start us, length us, event | category | flops | bytes accessed | tf_op | source)
XLA Modules:
  0.0 394.7 jit_solution(1865737707075941602)
XLA Ops:
  7.2 0.0 copy-start
  7.2 0.0 copy-start.4
  7.2 0.0 reduce-scatter.2.cloned.1.call-start
  7.2 4.4 %collective-permute-start.1 = (bf16[64,128]{1,0:T(8,128)(2,1)}, bf16[64,128]{1,0:T(8,128)(2,1)S(1)}, u32[]{:S(2)}, u32[]{:S(2)}) collective-permute-start(bf16[64,128]{1,0:T(8,128)(2,1)} %param.11), channel_id=1, source_target_pairs={{0,1},{1,0},{2,3},{3,2},{4,5},{5,4},{6,7},{7,6},{8,9},{9,8},{10,11... | collective-permute-start | bytes 49160 | tf_op jit(solution)/shard_map/ppermute | solution.py:37
  11.7 1.9 collective-permute-done.1
  13.6 0.8 maximum_select_fusion.7
  14.4 6.1 %collective-permute-start.2 = (bf16[128,128]{1,0:T(8,128)(2,1)S(1)}, bf16[128,128]{1,0:T(8,128)(2,1)S(1)}, u32[]{:S(2)}, u32[]{:S(2)}) collective-permute-start(bf16[128,128]{1,0:T(8,128)(2,1)S(1)} %maximum_select_fusion.7), channel_id=1, source_target_pairs={{0,2},{1,3},{2,0},{3,1},{4,6},{5,7},{6,4},{7,5},{8,10},{9,11},{10,... | collective-permute-start | bytes 98312 | tf_op jit(solution)/shard_map/ppermute | solution.py:37
  20.5 0.7 fusion.27
  21.1 1.2 collective-permute-done.2
  22.4 9.3 %collective-permute-start.3 = (bf16[256,128]{1,0:T(8,128)(2,1)S(1)}, bf16[256,128]{1,0:T(8,128)(2,1)S(1)}, u32[]{:S(2)}, u32[]{:S(2)}) collective-permute-start(bf16[256,128]{1,0:T(8,128)(2,1)S(1)} %maximum_select_fusion.6), channel_id=1, source_target_pairs={{0,4},{1,5},{2,6},{3,7},{4,0},{5,1},{6,2},{7,3},{8,12},{9,13},{10,... | collective-permute-start | bytes 196616 | tf_op jit(solution)/shard_map/ppermute | solution.py:37
  31.7 1.9 fusion.14
  33.6 2.2 collective-permute-start
  35.8 0.0 collective-permute-done.3
  35.9 0.0 copy-start.5
  35.9 3.6 collective-permute-start.4
  39.5 0.0 copy-done
  39.5 0.0 copy-done.4
  39.5 2.7 fusion.16
  42.2 19.6 %collective-permute-done.4 = bf16[512,128]{1,0:T(8,128)(2,1)S(1)} collective-permute-done((bf16[512,128]{1,0:T(8,128)(2,1)S(1)}, bf16[512,128]{1,0:T(8,128)(2,1)S(1)}, u32[]{:S(2)}, u32[]{:S(2)}) %collective-permute-start.4) | collective-permute-done | bytes 131104 | tf_op jit(solution)/shard_map/ppermute | solution.py:37
  61.8 0.1 maximum_select_fusion.2
  61.9 1.9 collective-permute-start.5
  63.8 0.0 copy-done.5
  63.8 4.9 %convolution_add_fusion.2 = f32[256,4096]{1,0:T(8,128)} fusion(f32[256,4096]{1,0:T(8,128)} %fusion.16, bf16[256,128]{1,0:T(8,128)(2,1)S(1)} %copy-done.5, bf16[1,128,4096]{2,1,0:T(8,128)(2,1)S(1)} %copy-done), kind=kOutput, calls=%fused_computation.4 | convolution fusion | flops 269484032 | bytes 9502720 | tf_op jit(solution)/shard_map/dot_general | solution.py:18
  68.7 2.9 collective-permute-done.5
  71.6 0.1 maximum_select_fusion.1
  71.8 7.5 %collective-permute-start.6 = (bf16[2048,128]{1,0:T(8,128)(2,1)S(1)}, bf16[2048,128]{1,0:T(8,128)(2,1)S(1)}, u32[]{:S(2)}, u32[]{:S(2)}) collective-permute-start(bf16[2048,128]{1,0:T(8,128)(2,1)S(1)} %maximum_select_fusion.1), channel_id=1, source_target_pairs={{0,32},{1,33},{2,34},{3,35},{4,36},{5,37},{6,38},{7,39},{8,40},{9,... | collective-permute-start | bytes 1572872 | tf_op jit(solution)/shard_map/ppermute | solution.py:37
  79.2 2.7 fusion.43
  81.9 0.7 fusion.42
  82.6 13.8 %collective-permute-done.6 = bf16[2048,128]{1,0:T(8,128)(2,1)S(1)} collective-permute-done((bf16[2048,128]{1,0:T(8,128)(2,1)S(1)}, bf16[2048,128]{1,0:T(8,128)(2,1)S(1)}, u32[]{:S(2)}, u32[]{:S(2)}) %collective-permute-start.6) | collective-permute-done | bytes 524320 | tf_op jit(solution)/shard_map/ppermute | solution.py:37
  96.4 0.7 fusion.18
  97.1 0.0 copy-start.7
  97.1 2.7 fusion.2
  99.8 0.0 copy-start.6
  99.8 0.0 collective-permute-done
  99.8 0.0 copy-done.7
  99.8 0.0 copy-start.3
  99.8 2.1 convolution_add_fusion.1
  101.9 0.0 copy-done.6
  101.9 0.4 copy-done.3
  102.4 0.0 copy-start.2
  102.4 4.1 %fusion.1 = f32[256,4096]{1,0:T(8,128)} fusion(f32[4096,256]{0,1:T(8,128)S(1)} %convolution_add_fusion.1, f32[4096,256]{0,1:T(8,128)S(1)} %copy-done.3, bf16[256,128]{1,0:T(8,128)(2,1)S(1)} %copy-done.6, bf16[128,4096]{1,0:T(8,128)(2,1)} %collective-permute-done), kind=kOutput, calls=%fused_computation.2 | convolution fusion | flops 270532608 | bytes 13697024 | tf_op jit(solution)/shard_map/dot_general | solution.py:18
  106.5 0.0 copy-done.2
  106.5 6.2 %multiply_add_fusion = (f32[128,4096]{1,0:T(8,128)S(1)}, f32[128,4096]{1,0:T(8,128)S(1)}, f32[128,4096]{1,0:T(8,128)S(1)}, f32[128,4096]{1,0:T(8,128)}) fusion(f32[256,4096]{1,0:T(8,128)S(1)} %copy-done.2, f32[256,4096]{1,0:T(8,128)} %fusion.1, f32[256,4096]{1,0:T(8,128)} %fusion.2), kind=kLoop, calls=%fused_computation.23 | loop fusion | flops 6291456 | bytes 20971520 | tf_op jit(solution)/shard_map/add | solution.py:61
  112.7 0.8 fusion.11
  113.4 0.8 fusion.25
  114.2 2.1 fusion.4
  116.3 0.0 reduce-scatter.2.cloned.1.call-update
  116.3 0.0 copy-start.1
  116.3 2.5 fusion.10
  118.8 0.0 copy-done.1
  118.8 0.8 fusion.21
  119.7 1.9 fusion.7
  121.6 2.3 copy.9
  123.8 239.3 %reduce-scatter.2.cloned.1.call-done = f32[64,128]{1,0:T(8,128)} async-done(((f32[4096,128]{1,0:T(8,128)}), f32[64,128]{1,0:T(8,128)}) %reduce-scatter.2.cloned.1.call-update) | async-done | bytes 32784 | tf_op jit(solution)/shard_map/reduce_scatter | solution.py:64
  363.1 24.7 %psum.7 = f32[64,128]{1,0:T(8,128)} all-reduce(f32[64,128]{1,0:T(8,128)} %reduce-scatter.2.cloned.1.call-done), channel_id=1, replica_groups=mesh['dp'=8,'ctx'=64] {'dp'}, use_global_device_ids=true, to_apply=%region_1.2 | all-reduce | flops 8192 | bytes 65536 | tf_op jit(solution)/shard_map/psum | solution.py:64
  (2 shorter events, 0.1 us)
Async XLA Ops:
  7.2 32.3 %copy-start = (bf16[1,128,4096]{2,1,0:T(8,128)(2,1)S(1)}, bf16[1,128,4096]{2,1,0:T(8,128)(2,1)}, u32[]{:S(2)}) copy-start(bf16[1,128,4096]{2,1,0:T(8,128)(2,1)} %param.9) | copy-start | bytes 3145732
  7.2 32.3 %copy-start.4 = (bf16[256,128]{1,0:T(8,128)(2,1)S(1)}, bf16[256,128]{1,0:T(8,128)(2,1)}, u32[]{:S(2)}) copy-start(bf16[256,128]{1,0:T(8,128)(2,1)} %constant.37) | copy-start | bytes 196612
  7.2 355.9 %reduce-scatter.2.cloned.1.call-start = ((), (), s32[]{:S(2)}) async-start(), calls=%async_computation.1 | async-start | bytes 2129920 | tf_op jit(solution)/shard_map/reduce_scatter | solution.py:64
  7.2 6.3 %collective-permute-start.1 = (bf16[64,128]{1,0:T(8,128)(2,1)}, bf16[64,128]{1,0:T(8,128)(2,1)S(1)}, u32[]{:S(2)}, u32[]{:S(2)}) collective-permute-start(bf16[64,128]{1,0:T(8,128)(2,1)} %param.11), channel_id=1, source_target_pairs={{0,1},{1,0},{2,3},{3,2},{4,5},{5,4},{6,7},{7,6},{8,9},{9,8},{10,11... | collective-permute-start | bytes 49160 | tf_op jit(solution)/shard_map/ppermute | solution.py:37
  14.4 8.0 %collective-permute-start.2 = (bf16[128,128]{1,0:T(8,128)(2,1)S(1)}, bf16[128,128]{1,0:T(8,128)(2,1)S(1)}, u32[]{:S(2)}, u32[]{:S(2)}) collective-permute-start(bf16[128,128]{1,0:T(8,128)(2,1)S(1)} %maximum_select_fusion.7), channel_id=1, source_target_pairs={{0,2},{1,3},{2,0},{3,1},{4,6},{5,7},{6,4},{7,5},{8,10},{9,11},{10,... | collective-permute-start | bytes 98312 | tf_op jit(solution)/shard_map/ppermute | solution.py:37
  22.4 13.4 %collective-permute-start.3 = (bf16[256,128]{1,0:T(8,128)(2,1)S(1)}, bf16[256,128]{1,0:T(8,128)(2,1)S(1)}, u32[]{:S(2)}, u32[]{:S(2)}) collective-permute-start(bf16[256,128]{1,0:T(8,128)(2,1)S(1)} %maximum_select_fusion.6), channel_id=1, source_target_pairs={{0,4},{1,5},{2,6},{3,7},{4,0},{5,1},{6,2},{7,3},{8,12},{9,13},{10,... | collective-permute-start | bytes 196616 | tf_op jit(solution)/shard_map/ppermute | solution.py:37
  33.6 66.2 %collective-permute-start = (bf16[128,4096]{1,0:T(8,128)(2,1)S(1)}, bf16[128,4096]{1,0:T(8,128)(2,1)}, u32[]{:S(2)}, u32[]{:S(2)}) collective-permute-start(bf16[128,4096]{1,0:T(8,128)(2,1)S(1)} %fusion.14), channel_id=1, source_target_pairs={{1,0},{2,1},{3,2},{4,3},{5,4},{6,5},{7,6},{8,7},{9,8},{10,9},{11,1... | collective-permute-start | bytes 3145736 | tf_op jit(solution)/shard_map/ppermute | solution.py:42
  35.9 28.0 %copy-start.5 = (bf16[256,128]{1,0:T(8,128)(2,1)S(1)}, bf16[256,128]{1,0:T(8,128)(2,1)}, u32[]{:S(2)}) copy-start(bf16[256,128]{1,0:T(8,128)(2,1)} %constant.39) | copy-start | bytes 196612
  35.9 25.9 %collective-permute-start.4 = (bf16[512,128]{1,0:T(8,128)(2,1)S(1)}, bf16[512,128]{1,0:T(8,128)(2,1)S(1)}, u32[]{:S(2)}, u32[]{:S(2)}) collective-permute-start(bf16[512,128]{1,0:T(8,128)(2,1)S(1)} %maximum_select_fusion.5), channel_id=1, source_target_pairs={{0,8},{1,9},{2,10},{3,11},{4,12},{5,13},{6,14},{7,15},{8,0},{9,1},... | collective-permute-start | bytes 393224 | tf_op jit(solution)/shard_map/ppermute | solution.py:37
  61.9 9.7 %collective-permute-start.5 = (bf16[1024,128]{1,0:T(8,128)(2,1)S(1)}, bf16[1024,128]{1,0:T(8,128)(2,1)S(1)}, u32[]{:S(2)}, u32[]{:S(2)}) collective-permute-start(bf16[1024,128]{1,0:T(8,128)(2,1)S(1)} %maximum_select_fusion.2), channel_id=1, source_target_pairs={{0,16},{1,17},{2,18},{3,19},{4,20},{5,21},{6,22},{7,23},{8,24},{9,... | collective-permute-start | bytes 786440 | tf_op jit(solution)/shard_map/ppermute | solution.py:37
  71.8 24.6 %collective-permute-start.6 = (bf16[2048,128]{1,0:T(8,128)(2,1)S(1)}, bf16[2048,128]{1,0:T(8,128)(2,1)S(1)}, u32[]{:S(2)}, u32[]{:S(2)}) collective-permute-start(bf16[2048,128]{1,0:T(8,128)(2,1)S(1)} %maximum_select_fusion.1), channel_id=1, source_target_pairs={{0,32},{1,33},{2,34},{3,35},{4,36},{5,37},{6,38},{7,39},{8,40},{9,... | collective-permute-start | bytes 1572872 | tf_op jit(solution)/shard_map/ppermute | solution.py:37
  97.1 2.7 copy-start.7
  99.8 2.1 copy-start.6
  99.8 2.5 copy-start.3
  102.4 4.2 %copy-start.2 = (f32[256,4096]{1,0:T(8,128)S(1)}, f32[256,4096]{1,0:T(8,128)}, u32[]{:S(2)}) copy-start(f32[256,4096]{1,0:T(8,128)} %convolution_add_fusion.2) | copy-start | bytes 12582916
  116.3 2.5 copy-start.1
Sparse Core Ops, SparseCore 0:
  116.4 246.6 reduce-scatter.1
